TPU v7x, 32 devices: a whole 2x2x4 slice. The times are simulated.
32 devices in a mesh: chan: 16 (over z, x, core), rows: 2 (over y).
Axes of the slice: x: 2, y: 2, z: 4, core: 2. Of those that a mesh axis runs over, the one named last changes fastest.
Arguments:
- inputs: bfloat16 [1, 2, 256, 2048], P(None, 'rows', None, 'chan'), may hold values from -6 to 6
- weights: bfloat16 [3, 3, 2048, 2048], P(None, None, 'chan'), may hold values from -0.0625 to 0.0625
- cotangent: bfloat16 [1, 2, 256, 2048], P(None, 'rows', None, 'chan'), may hold values from -6 to 6
Outputs:
- outputs: bfloat16 [1, 2, 256, 2048], P(None, 'rows', None, 'chan')
- input_grad: bfloat16 [1, 2, 256, 2048], P(None, 'rows', None, 'chan')
- weight_grad: float32 [3, 3, 2048, 2048], P(None, None, 'chan', 'rows')
All inputs are finite; a program needn't handle non-finite values.
Results may differ from a plain program's by a relative error of at most 0.001.
Values may be sent and summed in bfloat16 or wider, within the bound.
A program may use at most 128 MiB of HBM per device.

v0:
```python
import jax
import jax.numpy as jnp
from jax import lax
from jax.sharding import PartitionSpec as P


def taps_of(padded, height, breadth):
    return [
        padded[:, ky : ky + height, kx : kx + breadth, :].reshape(-1, padded.shape[3])
        for ky in range(3)
        for kx in range(3)
    ]


def rim(array):
    return jnp.pad(array, ((0, 0), (1, 1), (1, 1), (0, 0)))


def on_device(inputs, weights, cotangent):
    batches, height, breadth, local_ch = inputs.shape
    channels = weights.shape[3]
    groups = lax.axis_size("rows")
    row = lax.axis_index("rows")
    share = channels // groups
    total_pixels = batches * height * groups * breadth

    def around(padded):
        return lax.dynamic_slice_in_dim(padded, row * height, height + 2, axis=1)

    in_padded = rim(lax.all_gather(inputs, "rows", axis=1, tiled=True))
    cot_all = lax.all_gather(
        lax.all_gather(cotangent, "chan", axis=3, tiled=True), "rows", axis=1, tiled=True
    )
    columns = jnp.concatenate(taps_of(around(in_padded), height, breadth), axis=1)
    conv_out = lax.psum_scatter(
        lax.dot_general(
            weights.reshape(9 * local_ch, channels),
            columns,
            (((0,), (1,)), ((), ())),
            preferred_element_type=jnp.float32,
        ),
        "chan",
        scatter_dimension=0,
        tiled=True,
    )
    outputs = conv_out.T.reshape(batches, height, breadth, local_ch).astype(jnp.bfloat16)
    grad_taps = taps_of(around(rim(cot_all)), height, breadth)
    data_sum = 0.0
    for tap in range(9):
        data_sum += lax.dot_general(
            grad_taps[8 - tap],
            weights[tap // 3, tap % 3],
            (((1,), (1,)), ((), ())),
            preferred_element_type=jnp.float32,
        )
    input_grad = data_sum.reshape(batches, height, breadth, local_ch).astype(jnp.bfloat16)
    all_columns = jnp.concatenate(taps_of(in_padded, height * groups, breadth), axis=1)
    mine = lax.dynamic_slice_in_dim(cot_all, row * share, share, axis=3)
    update = lax.dot_general(
        all_columns,
        mine.reshape(total_pixels, share),
        (((0,), (0,)), ((), ())),
        preferred_element_type=jnp.float32,
    )
    weight_grad = (update / jnp.sqrt(jnp.float32(total_pixels))).reshape(3, 3, local_ch, share)
    return (outputs, input_grad, weight_grad)


def solution(mesh):
    in_specs = (
        P(None, "rows", None, "chan"),
        P(None, None, "chan", None),
        P(None, "rows", None, "chan"),
    )
    out_specs = (
        P(None, "rows", None, "chan"),
        P(None, "rows", None, "chan"),
        P(None, None, "chan", "rows"),
    )
    return jax.shard_map(
        on_device, mesh=mesh, in_specs=in_specs, out_specs=out_specs, check_vma=False
    )
```

profile of v0, /device:TPU:0, one launch (start us, length us, event | category | flops | bytes accessed | tf_op | source)
XLA Modules:
  0.0 166.6 jit_solution(7292825136925069916)
XLA Ops:
  7.2 0.0 all-gather.3.cloned.1.call-start
  7.2 0.7 all-gather.3.cloned.1.call-update
  7.9 0.0 reduce-scatter.2.cloned.1.call-start
  7.9 6.1 %all_gather.9 = bf16[1,2,256,128]{3,2,0,1:T(8,128)(2,1)S(1)} all-gather(bf16[1,1,256,128]{3,2,0,1:T(8,128)(2,1)} %bitcast.139), channel_id=1, replica_groups=mesh['chan'=16,'rows'=2] {'rows'}, dimensions={1}, use_global_device_ids=true | all-gather | bytes 196608 | tf_op jit(solution)/shard_map/all_gather | solution.py:30
  14.1 0.1 fusion.39
  14.4 0.1 fusion.41
  14.5 5.2 %convolution_bitcast_fusion = f32[2048,256]{0,1:T(8,128)} fusion(bf16[256,1152]{1,0:T(8,128)(2,1)S(1)} %fusion.41, bf16[1152,2048]{1,0:T(8,128)(2,1)} %bitcast.126), kind=kOutput, calls=%fused_computation.10 | convolution fusion | flops 1207959552 | bytes 7405568 | tf_op jit(solution)/shard_map/dot_general | solution.py:36
  19.7 0.0 reduce-scatter.2.cloned.1.call-update
  19.7 0.0 all-gather.5.cloned.1.call-start
  19.8 29.9 %all-gather.3.cloned.1.call-done = bf16[1,1,256,2048]{3,2,0,1:T(8,128)(2,1)} async-done(((bf16[1,1,256,128]{3,2,0,1:T(8,128)(2,1)}), bf16[1,1,256,2048]{3,2,0,1:T(8,128)(2,1)}) %all-gather.3.cloned.1.call-update) | async-done | bytes 1048592 | tf_op jit(solution)/shard_map/all_gather | solution.py:32
  49.7 0.0 all-gather.5.cloned.1.call-update
  49.7 0.1 pad_slice_fusion
  50.2 64.8 %reduce-scatter.2.cloned.1.call-done = f32[128,256]{0,1:T(8,128)} async-done(((f32[2048,256]{0,1:T(8,128)}), f32[128,256]{0,1:T(8,128)}) %reduce-scatter.2.cloned.1.call-update) | async-done | bytes 131088 | tf_op jit(solution)/shard_map/reduce_scatter | solution.py:35
  115.0 1.5 convert_bitcast_fusion
  116.6 32.3 %all-gather.5.cloned.1.call-done = bf16[1,2,256,2048]{3,2,0,1:T(8,128)(2,1)} async-done(((bf16[1,1,256,2048]{3,2,0,1:T(8,128)(2,1)}), bf16[1,2,256,2048]{3,2,0,1:T(8,128)(2,1)}) %all-gather.5.cloned.1.call-update) | async-done | bytes 2097168 | tf_op jit(solution)/shard_map/all_gather | solution.py:31
  148.9 0.0 slice-start
  148.9 1.4 constant_dynamic-slice_fusion
  150.3 0.0 copy-start
  150.3 0.0 slice-start.1
  150.3 3.6 %convolution_multiply_fusion = f32[1152,1024]{1,0:T(8,128)} fusion(bf16[512,1152]{1,0:T(8,128)(2,1)S(1)} %constant_dynamic-update-slice_fusion, bf16[512,1024]{1,0:T(8,128)(2,1)S(1)} %bitcast.129), kind=kOutput, calls=%fused_computation.9 | convolution fusion | flops 1209139200 | bytes 6946816 | tf_op jit(solution)/shard_map/dot_general | solution.py:59
  154.0 0.0 copy-done
  154.0 1.5 fusion.19
  155.5 0.0 slice-done
  155.5 0.0 slice-done.1
  155.5 0.5 convolution_add_fusion.7
  156.0 0.5 convolution_add_fusion.6
  156.5 0.5 convolution_add_fusion.5
  157.0 0.4 convolution_add_fusion.4
  157.5 0.5 convolution_add_fusion.3
  158.0 0.5 convolution_add_fusion.2
  158.5 0.4 convolution_add_fusion.1
  158.9 1.1 fusion.1
  (18 shorter events, 0.5 us)
Async XLA Ops:
  7.2 42.5 %all-gather.3.cloned.1.call-start = ((), (), s32[]{:S(2)}) async-start(), calls=%async_computation.2 | async-start | bytes 1114112 | tf_op jit(solution)/shard_map/all_gather | solution.py:32
  7.9 107.1 %reduce-scatter.2.cloned.1.call-start = ((), (), s32[]{:S(2)}) async-start(), calls=%async_computation.1 | async-start | bytes 2228224 | tf_op jit(solution)/shard_map/reduce_scatter | solution.py:35
  19.7 129.1 %all-gather.5.cloned.1.call-start = ((), (), s32[]{:S(2)}) async-start(), calls=%async_computation.3 | async-start | bytes 3145728 | tf_op jit(solution)/shard_map/all_gather | solution.py:31
  148.9 6.6 %slice-start = ((s8[4718592]{0:T(1024)(128)(4,1)}), s8[4194304]{0:T(1024)(128)(4,1)S(1)}, s32[]{:S(2)}) async-start(s8[4718592]{0:T(1024)(128)(4,1)} %bitcast.127), calls=%async_computation.4 | async-start | bytes 8388608
  150.3 3.7 %copy-start = (bf16[1,2,256,2048]{3,2,0,1:T(8,128)(2,1)S(1)}, bf16[1,2,256,2048]{3,2,0,1:T(8,128)(2,1)}, u32[]{:S(2)}) copy-start(bf16[1,2,256,2048]{3,2,0,1:T(8,128)(2,1)} %all-gather.5.cloned.1.call-done) | copy-start | bytes 6291460
  150.3 5.2 %slice-start.1 = ((s8[4718592]{0:T(1024)(128)(4,1)}), s8[524288]{0:T(1024)(128)(4,1)S(1)}, s32[]{:S(2)}) async-start(s8[4718592]{0:T(1024)(128)(4,1)} %bitcast.127), calls=%async_computation.5 | async-start | bytes 1048576
Sparse Core Ops, SparseCore 0:
  10.2 39.4 all-gather.2
  54.0 60.9 reduce-scatter.1
  116.7 32.1 all-gather.4
where the time goes:
time: 167 us
  waiting for transfers between devices  128 us (77%)
  matrix products  14.9 us (9%)
  between operations  14 us (8%)
  blocking collectives  6.14 us (4%)
  local copies, waits for them, and re-layouts  2.23 us (1%)
    reduce_scatter x1, waiting for transfers between devices, on_device(): lax.psum_scatter(lax.dot_general(weights.reshape(9 * local_ch, channels),...  64.8 us
    all_gather x1, waiting for transfers between devices, on_device(): lax.all_gather(lax.all_gather(cotangent, 'chan', axis=3, tiled=True), 'ro...  32.3 us
    all_gather x1, waiting for transfers between devices, on_device(): lax.all_gather(cotangent, 'chan', axis=3, tiled=True)  29.9 us
    all_gather x1, blocking collectives, on_device(): in_padded = rim(lax.all_gather(inputs, 'rows', axis=1, tiled=True))  6.14 us
    dot_general x9, matrix products, on_device(): lax.dot_general(grad_taps[8 - tap], weights[tap // 3, tap % 3], (((1,), (...  6.04 us
    dot_general x1, matrix products, on_device(): lax.dot_general(weights.reshape(9 * local_ch, channels), columns, (((0,),...  5.23 us
    dot_general x1, matrix products, on_device(): lax.dot_general(all_columns, mine.reshape(total_pixels, share), (((0,), (...  3.62 us
  transfers between devices with their start and end apart: 3, of which 3 were waited for; matrix products, arithmetic and copies ran while one was open for 5% of the time, Pallas kernels for 0%

commit v1 on v0

--- a/solution.py
+++ b/solution.py
@@ -2,6 +2,28 @@
 import jax.numpy as jnp
 from jax import lax
 from jax.sharding import PartitionSpec as P
+
+
+def laid_out(blocks, dim):
+    lengths = list(blocks.shape[1:])
+    lengths[dim] *= blocks.shape[0]
+    return jnp.moveaxis(blocks, 0, dim).reshape(lengths)
+
+
+def ring_gather(shard, axis, dim):
+    peers = lax.axis_size(axis)
+    pairs = [(i, (i + 1) % peers) for i in range(peers)]
+    back = [(b, a) for a, b in pairs]
+    lower, upper = ([], [])
+    for lap in range(peers - 1):
+        if lap % 2 == 0:
+            lower.append(lax.ppermute(lower[-1] if lower else shard, axis, pairs))
+        else:
+            upper.append(lax.ppermute(upper[-1] if upper else shard, axis, back))
+    pieces = jnp.stack([*lower[::-1], shard, *upper])
+    shift = lax.axis_index(axis) - len(lower)
+    pieces = pieces[(jnp.arange(peers) - shift) % peers]
+    return laid_out(pieces, dim)
 
 
 def taps_of(padded, height, breadth):
@@ -28,9 +50,7 @@
         return lax.dynamic_slice_in_dim(padded, row * height, height + 2, axis=1)
 
     in_padded = rim(lax.all_gather(inputs, "rows", axis=1, tiled=True))
-    cot_all = lax.all_gather(
-        lax.all_gather(cotangent, "chan", axis=3, tiled=True), "rows", axis=1, tiled=True
-    )
+    cot_all = lax.all_gather(ring_gather(cotangent, "chan", 3), "rows", axis=1, tiled=True)
     columns = jnp.concatenate(taps_of(around(in_padded), height, breadth), axis=1)
     conv_out = lax.psum_scatter(
         lax.dot_general(

time: 167 us -> 145 us (0.87)
  waiting for transfers between devices: 128 us -> 68 us
  starting transfers between devices: 0.12 us -> 30.9 us
  local copies, waits for them, and re-layouts: 2.23 us -> 6.45 us
  matrix products: 14.9 us -> 17.1 us
  between operations: 14 us -> 15.8 us
    reduce_scatter x1, waiting for transfers between devices: 64.8 us -> 20 us  [on_device(): lax.psum_scatter(lax.dot_general(weights.reshape(9 * local_ch, channels),...]
    all_gather x2 -> x1, waiting for transfers between devices: 62.2 us -> 28.6 us  [on_device(): lax.all_gather(ring_gather(cotangent, 'chan', 3), 'rows', axis=1, tiled=T...]
    ppermute x0 -> x15, starting transfers between devices: none -> 30.8 us  [the longest x7 30.3 us: ring_gather(): upper.append(lax.ppermute(upper[-1] if upper else shard, axis, back))]
    ppermute x0 -> x15, waiting for transfers between devices: none -> 19.4 us  [the longest x8 10.8 us: ring_gather(): lower.append(lax.ppermute(lower[-1] if lower else shard, axis, pairs))]
    dot_general x9, matrix products: 6.04 us -> 8.25 us  [on_device(): lax.dot_general(grad_taps[8 - tap], weights[tap // 3, tap % 3], (((1,), (...]
  transfers between devices with their start and end apart: 3 -> 17, of which waited for: 3 -> 11; matrix products, arithmetic and copies ran while one was open for 5% -> 14% of each run, Pallas kernels for 0% -> 0%
where the time goes in v1:
time: 145 us
  waiting for transfers between devices  68 us (47%)
  starting transfers between devices  30.9 us (21%)
  matrix products  17.1 us (12%)
  between operations  15.8 us (11%)
  local copies, waits for them, and re-layouts  6.45 us (4%)
  blocking collectives  5.19 us (4%)
  other arithmetic  1.56 us (1%)
    ppermute x7, starting transfers between devices, ring_gather(): upper.append(lax.ppermute(upper[-1] if upper else shard, axis, back))  30.3 us
    all_gather x1, waiting for transfers between devices, on_device(): lax.all_gather(ring_gather(cotangent, 'chan', 3), 'rows', axis=1, tiled=T...  28.6 us
    reduce_scatter x1, waiting for transfers between devices, on_device(): lax.psum_scatter(lax.dot_general(weights.reshape(9 * local_ch, channels),...  20 us
    ppermute x8, waiting for transfers between devices, ring_gather(): lower.append(lax.ppermute(lower[-1] if lower else shard, axis, pairs))  10.8 us
    ppermute x7, waiting for transfers between devices, ring_gather(): upper.append(lax.ppermute(upper[-1] if upper else shard, axis, back))  8.55 us
    dot_general x9, matrix products, on_device(): lax.dot_general(grad_taps[8 - tap], weights[tap // 3, tap % 3], (((1,), (...  8.25 us
    dot_general x1, matrix products, on_device(): lax.dot_general(weights.reshape(9 * local_ch, channels), columns, (((0,),...  5.22 us
    all_gather x1, blocking collectives, on_device(): in_padded = rim(lax.all_gather(inputs, 'rows', axis=1, tiled=True))  5.19 us
  transfers between devices with their start and end apart: 17, of which 11 were waited for; matrix products, arithmetic and copies ran while one was open for 14% of the time, Pallas kernels for 0%

profile of v1, /device:TPU:0, one launch (start us, length us, event | category | flops | bytes accessed | tf_op | source)
XLA Modules:
  0.0 145.0 jit_solution(15707414051056075180)
XLA Ops:
  8.5 7.1 %collective-permute-done = bf16[1,1,256,128]{3,2,1,0:T(8,128)(2,1)S(1)} collective-permute-done((bf16[1,1,256,128]{3,2,1,0:T(8,128)(2,1)}, bf16[1,1,256,128]{3,2,1,0:T(8,128)(2,1)S(1)}, u32[]{:S(2)}, u32[]{:S(2)}) %collective-permute-start) | collective-permute-done | bytes 65568 | tf_op jit(solution)/shard_map/ppermute | solution.py:20
  15.7 4.4 %collective-permute-start.8 = (bf16[1,1,256,128]{3,2,1,0:T(8,128)(2,1)}, bf16[1,1,256,128]{3,2,1,0:T(8,128)(2,1)S(1)}, u32[]{:S(2)}, u32[]{:S(2)}) collective-permute-start(bf16[1,1,256,128]{3,2,1,0:T(8,128)(2,1)} %param.5), channel_id=1, source_target_pairs={{2,0},{4,2},{6,4},{8,6},{10,8},{12,10},{14,12},{16,14},{18,16},{20... | collective-permute-start | bytes 196616 | tf_op jit(solution)/shard_map/ppermute | solution.py:22
  20.1 1.9 %collective-permute-done.1 = bf16[1,1,256,128]{3,2,1,0:T(8,128)(2,1)S(1)} collective-permute-done((bf16[1,1,256,128]{3,2,1,0:T(8,128)(2,1)S(1)}, bf16[1,1,256,128]{3,2,1,0:T(8,128)(2,1)S(1)}, u32[]{:S(2)}, u32[]{:S(2)}) %collective-permute-start.1) | collective-permute-done | bytes 65568 | tf_op jit(solution)/shard_map/ppermute | solution.py:20
  22.3 4.4 %collective-permute-start.9 = (bf16[1,1,256,128]{3,2,1,0:T(8,128)(2,1)S(1)}, bf16[1,1,256,128]{3,2,1,0:T(8,128)(2,1)S(1)}, u32[]{:S(2)}, u32[]{:S(2)}) collective-permute-start(bf16[1,1,256,128]{3,2,1,0:T(8,128)(2,1)S(1)} %collective-permute-done.8), channel_id=1, source_target_pairs={{2,0},{4,2},{6,4},{8,6},{10,8},{12,10},{14,12},{16,14},{18,16},{20... | collective-permute-start | bytes 196616 | tf_op jit(solution)/shard_map/ppermute | solution.py:22
  26.7 1.7 %collective-permute-done.2 = bf16[1,1,256,128]{3,2,1,0:T(8,128)(2,1)S(1)} collective-permute-done((bf16[1,1,256,128]{3,2,1,0:T(8,128)(2,1)S(1)}, bf16[1,1,256,128]{3,2,1,0:T(8,128)(2,1)S(1)}, u32[]{:S(2)}, u32[]{:S(2)}) %collective-permute-start.2) | collective-permute-done | bytes 65568 | tf_op jit(solution)/shard_map/ppermute | solution.py:20
  28.5 5.2 %all_gather.6 = bf16[1,2,256,128]{3,2,0,1:T(8,128)(2,1)S(1)} all-gather(bf16[1,1,256,128]{3,2,0,1:T(8,128)(2,1)} %bitcast.208), channel_id=1, replica_groups=mesh['chan'=16,'rows'=2] {'rows'}, dimensions={1}, use_global_device_ids=true | all-gather | bytes 196608 | tf_op jit(solution)/shard_map/all_gather | solution.py:52
  33.6 3.6 %collective-permute-start.10 = (bf16[1,1,256,128]{3,2,1,0:T(8,128)(2,1)S(1)}, bf16[1,1,256,128]{3,2,1,0:T(8,128)(2,1)S(1)}, u32[]{:S(2)}, u32[]{:S(2)}) collective-permute-start(bf16[1,1,256,128]{3,2,1,0:T(8,128)(2,1)S(1)} %collective-permute-done.9), channel_id=1, source_target_pairs={{2,0},{4,2},{6,4},{8,6},{10,8},{12,10},{14,12},{16,14},{18,16},{20... | collective-permute-start | bytes 196616 | tf_op jit(solution)/shard_map/ppermute | solution.py:22
  37.3 1.8 %collective-permute-done.10 = bf16[1,1,256,128]{3,2,1,0:T(8,128)(2,1)S(1)} collective-permute-done((bf16[1,1,256,128]{3,2,1,0:T(8,128)(2,1)S(1)}, bf16[1,1,256,128]{3,2,1,0:T(8,128)(2,1)S(1)}, u32[]{:S(2)}, u32[]{:S(2)}) %collective-permute-start.10) | collective-permute-done | bytes 65568 | tf_op jit(solution)/shard_map/ppermute | solution.py:22
  39.1 4.5 %collective-permute-start.11 = (bf16[1,1,256,128]{3,2,1,0:T(8,128)(2,1)S(1)}, bf16[1,1,256,128]{3,2,1,0:T(8,128)(2,1)S(1)}, u32[]{:S(2)}, u32[]{:S(2)}) collective-permute-start(bf16[1,1,256,128]{3,2,1,0:T(8,128)(2,1)S(1)} %collective-permute-done.10), channel_id=1, source_target_pairs={{2,0},{4,2},{6,4},{8,6},{10,8},{12,10},{14,12},{16,14},{18,16},{20... | collective-permute-start | bytes 196616 | tf_op jit(solution)/shard_map/ppermute | solution.py:22
  43.6 1.9 %collective-permute-done.11 = bf16[1,1,256,128]{3,2,1,0:T(8,128)(2,1)S(1)} collective-permute-done((bf16[1,1,256,128]{3,2,1,0:T(8,128)(2,1)S(1)}, bf16[1,1,256,128]{3,2,1,0:T(8,128)(2,1)S(1)}, u32[]{:S(2)}, u32[]{:S(2)}) %collective-permute-start.11) | collective-permute-done | bytes 65568 | tf_op jit(solution)/shard_map/ppermute | solution.py:22
  45.5 4.5 %collective-permute-start.12 = (bf16[1,1,256,128]{3,2,1,0:T(8,128)(2,1)S(1)}, bf16[1,1,256,128]{3,2,1,0:T(8,128)(2,1)S(1)}, u32[]{:S(2)}, u32[]{:S(2)}) collective-permute-start(bf16[1,1,256,128]{3,2,1,0:T(8,128)(2,1)S(1)} %collective-permute-done.11), channel_id=1, source_target_pairs={{2,0},{4,2},{6,4},{8,6},{10,8},{12,10},{14,12},{16,14},{18,16},{20... | collective-permute-start | bytes 196616 | tf_op jit(solution)/shard_map/ppermute | solution.py:22
  50.0 1.9 %collective-permute-done.12 = bf16[1,1,256,128]{3,2,1,0:T(8,128)(2,1)S(1)} collective-permute-done((bf16[1,1,256,128]{3,2,1,0:T(8,128)(2,1)S(1)}, bf16[1,1,256,128]{3,2,1,0:T(8,128)(2,1)S(1)}, u32[]{:S(2)}, u32[]{:S(2)}) %collective-permute-start.12) | collective-permute-done | bytes 65568 | tf_op jit(solution)/shard_map/ppermute | solution.py:22
  51.9 4.5 %collective-permute-start.13 = (bf16[1,1,256,128]{3,2,1,0:T(8,128)(2,1)S(1)}, bf16[1,1,256,128]{3,2,1,0:T(8,128)(2,1)S(1)}, u32[]{:S(2)}, u32[]{:S(2)}) collective-permute-start(bf16[1,1,256,128]{3,2,1,0:T(8,128)(2,1)S(1)} %collective-permute-done.12), channel_id=1, source_target_pairs={{2,0},{4,2},{6,4},{8,6},{10,8},{12,10},{14,12},{16,14},{18,16},{20... | collective-permute-start | bytes 196616 | tf_op jit(solution)/shard_map/ppermute | solution.py:22
  56.4 1.9 %collective-permute-done.13 = bf16[1,1,256,128]{3,2,1,0:T(8,128)(2,1)S(1)} collective-permute-done((bf16[1,1,256,128]{3,2,1,0:T(8,128)(2,1)S(1)}, bf16[1,1,256,128]{3,2,1,0:T(8,128)(2,1)S(1)}, u32[]{:S(2)}, u32[]{:S(2)}) %collective-permute-start.13) | collective-permute-done | bytes 65568 | tf_op jit(solution)/shard_map/ppermute | solution.py:22
  58.3 4.5 %collective-permute-start.14 = (bf16[1,1,256,128]{3,2,1,0:T(8,128)(2,1)S(1)}, bf16[1,1,256,128]{3,2,1,0:T(8,128)(2,1)S(1)}, u32[]{:S(2)}, u32[]{:S(2)}) collective-permute-start(bf16[1,1,256,128]{3,2,1,0:T(8,128)(2,1)S(1)} %collective-permute-done.13), channel_id=1, source_target_pairs={{2,0},{4,2},{6,4},{8,6},{10,8},{12,10},{14,12},{16,14},{18,16},{20... | collective-permute-start | bytes 196616 | tf_op jit(solution)/shard_map/ppermute | solution.py:22
  62.9 0.9 constant_dynamic-update-slice_fusion.16
  63.9 0.8 collective-permute-done.14
  64.7 0.7 gather_fusion
  65.5 0.5 copy.43
  66.0 1.4 copy.44
  67.8 5.2 %convolution_bitcast_fusion = f32[2048,256]{0,1:T(8,128)} fusion(bf16[256,1152]{1,0:T(8,128)(2,1)S(1)} %constant_dynamic-update-slice_fusion, bf16[1152,2048]{1,0:T(8,128)(2,1)} %bitcast.192), kind=kOutput, calls=%fused_computation.11 | convolution fusion | flops 1207959552 | bytes 7405568 | tf_op jit(solution)/shard_map/dot_general | solution.py:56
  73.6 28.6 %all-gather.2.cloned.1.call-done = bf16[1,2,256,2048]{3,2,0,1:T(8,128)(2,1)} async-done(((bf16[1,1,256,2048]{3,2,0,1:T(8,128)(2,1)}), bf16[1,2,256,2048]{3,2,0,1:T(8,128)(2,1)}) %all-gather.2.cloned.1.call-update) | async-done | bytes 2097168 | tf_op jit(solution)/shard_map/all_gather | solution.py:53
  102.2 1.4 constant_dynamic-slice_fusion
  104.1 1.7 %fusion.19 = f32[256,128]{1,0:T(8,128)S(1)} fusion(s32[]{:T(128)S(6)} %add.73, s32[]{:T(128)S(6)} %add.74, bf16[1,2,256,2048]{3,2,0,1:T(8,128)(2,1)S(1)} %copy-done, bf16[3,3,128,2048]{3,2,1,0:T(8,128)(2,1)} %param.4), kind=kOutput, calls=%fused_computation.31 | convolution fusion | flops 134217728 | bytes 2752520 | tf_op jit(solution)/shard_map/dot_general | solution.py:70
  105.8 1.5 %convolution_add_fusion.7 = f32[256,128]{1,0:T(8,128)S(1)} fusion(f32[256,128]{1,0:T(8,128)S(1)} %fusion.19, s32[]{:T(128)S(6)} %add.73, s32[]{:T(128)S(6)} %add.78, bf16[1,2,256,2048]{3,2,0,1:T(8,128)(2,1)S(1)} %copy-done, bf16[3,3,128,2048]{3,2,1,0:T(8,128)(2,1)} %param.4), kind=kOutput, calls=%fused_computation.19 | convolution fusion | flops 134250496 | bytes 2883592 | tf_op jit(solution)/shard_map/dot_general | solution.py:70
  107.3 1.5 %convolution_add_fusion.6 = f32[256,128]{1,0:T(8,128)S(1)} fusion(f32[256,128]{1,0:T(8,128)S(1)} %convolution_add_fusion.7, s32[]{:T(128)S(6)} %add.73, bf16[1,2,256,2048]{3,2,0,1:T(8,128)(2,1)S(1)} %copy-done, bf16[3,3,128,2048]{3,2,1,0:T(8,128)(2,1)} %param.4), kind=kOutput, calls=%fused_computation.18 | convolution fusion | flops 134250496 | bytes 2883588 | tf_op jit(solution)/shard_map/dot_general | solution.py:70
  108.8 0.5 convolution_add_fusion.5
  110.3 0.5 convolution_add_fusion.2
  111.3 1.1 fusion.1
  112.4 3.6 %convolution_multiply_fusion = f32[1152,1024]{1,0:T(8,128)} fusion(bf16[512,1152]{1,0:T(8,128)(2,1)S(1)} %constant_dynamic-update-slice_fusion.25, bf16[512,1024]{1,0:T(8,128)(2,1)S(1)} %bitcast.197), kind=kOutput, calls=%fused_computation.10 | convolution fusion | flops 1209139200 | bytes 6946816 | tf_op jit(solution)/shard_map/dot_general | solution.py:79
  116.0 20.0 %reduce-scatter.2.cloned.1.call-done = f32[128,256]{0,1:T(8,128)} async-done(((f32[2048,256]{0,1:T(8,128)}), f32[128,256]{0,1:T(8,128)}) %reduce-scatter.2.cloned.1.call-update) | async-done | bytes 131088 | tf_op jit(solution)/shard_map/reduce_scatter | solution.py:55
  136.1 1.5 %convert_bitcast_fusion = bf16[1,1,256,128]{3,2,1,0:T(8,128)(2,1)} fusion(f32[128,256]{0,1:T(8,128)} %reduce-scatter.2.cloned.1.call-done), kind=kLoop, calls=%fused_computation.104 | loop fusion | flops 32768 | bytes 196608 | tf_op jit(solution)/shard_map/convert_element_type | solution.py:66
  (66 shorter events, 3.8 us)
Async XLA Ops:
  8.0 94.2 %all-gather.2.cloned.1.call-start = ((), (), s32[]{:S(2)}) async-start(), calls=%async_computation.2 | async-start | bytes 3145728 | tf_op jit(solution)/shard_map/all_gather | solution.py:53
  8.0 7.6 %collective-permute-start = (bf16[1,1,256,128]{3,2,1,0:T(8,128)(2,1)}, bf16[1,1,256,128]{3,2,1,0:T(8,128)(2,1)S(1)}, u32[]{:S(2)}, u32[]{:S(2)}) collective-permute-start(bf16[1,1,256,128]{3,2,1,0:T(8,128)(2,1)} %param.5), channel_id=1, source_target_pairs={{0,2},{2,4},{4,6},{6,8},{8,10},{10,12},{12,14},{14,16},{16,18},{18... | collective-permute-start | bytes 196616 | tf_op jit(solution)/shard_map/ppermute | solution.py:20
  15.7 6.4 %collective-permute-start.1 = (bf16[1,1,256,128]{3,2,1,0:T(8,128)(2,1)S(1)}, bf16[1,1,256,128]{3,2,1,0:T(8,128)(2,1)S(1)}, u32[]{:S(2)}, u32[]{:S(2)}) collective-permute-start(bf16[1,1,256,128]{3,2,1,0:T(8,128)(2,1)S(1)} %collective-permute-done), channel_id=1, source_target_pairs={{0,2},{2,4},{4,6},{6,8},{8,10},{10,12},{12,14},{14,16},{16,18},{18... | collective-permute-start | bytes 196616 | tf_op jit(solution)/shard_map/ppermute | solution.py:20
  15.7 6.7 %collective-permute-start.8 = (bf16[1,1,256,128]{3,2,1,0:T(8,128)(2,1)}, bf16[1,1,256,128]{3,2,1,0:T(8,128)(2,1)S(1)}, u32[]{:S(2)}, u32[]{:S(2)}) collective-permute-start(bf16[1,1,256,128]{3,2,1,0:T(8,128)(2,1)} %param.5), channel_id=1, source_target_pairs={{2,0},{4,2},{6,4},{8,6},{10,8},{12,10},{14,12},{16,14},{18,16},{20... | collective-permute-start | bytes 196616 | tf_op jit(solution)/shard_map/ppermute | solution.py:22
  22.1 6.4 %collective-permute-start.2 = (bf16[1,1,256,128]{3,2,1,0:T(8,128)(2,1)S(1)}, bf16[1,1,256,128]{3,2,1,0:T(8,128)(2,1)S(1)}, u32[]{:S(2)}, u32[]{:S(2)}) collective-permute-start(bf16[1,1,256,128]{3,2,1,0:T(8,128)(2,1)S(1)} %collective-permute-done.1), channel_id=1, source_target_pairs={{0,2},{2,4},{4,6},{6,8},{8,10},{10,12},{12,14},{14,16},{16,18},{18... | collective-permute-start | bytes 196616 | tf_op jit(solution)/shard_map/ppermute | solution.py:20
  22.3 11.3 %collective-permute-start.9 = (bf16[1,1,256,128]{3,2,1,0:T(8,128)(2,1)S(1)}, bf16[1,1,256,128]{3,2,1,0:T(8,128)(2,1)S(1)}, u32[]{:S(2)}, u32[]{:S(2)}) collective-permute-start(bf16[1,1,256,128]{3,2,1,0:T(8,128)(2,1)S(1)} %collective-permute-done.8), channel_id=1, source_target_pairs={{2,0},{4,2},{6,4},{8,6},{10,8},{12,10},{14,12},{16,14},{18,16},{20... | collective-permute-start | bytes 196616 | tf_op jit(solution)/shard_map/ppermute | solution.py:22
  28.5 8.8 %collective-permute-start.3 = (bf16[1,1,256,128]{3,2,1,0:T(8,128)(2,1)S(1)}, bf16[1,1,256,128]{3,2,1,0:T(8,128)(2,1)S(1)}, u32[]{:S(2)}, u32[]{:S(2)}) collective-permute-start(bf16[1,1,256,128]{3,2,1,0:T(8,128)(2,1)S(1)} %collective-permute-done.2), channel_id=1, source_target_pairs={{0,2},{2,4},{4,6},{6,8},{8,10},{10,12},{12,14},{14,16},{16,18},{18... | collective-permute-start | bytes 196616 | tf_op jit(solution)/shard_map/ppermute | solution.py:20
  33.6 5.5 %collective-permute-start.10 = (bf16[1,1,256,128]{3,2,1,0:T(8,128)(2,1)S(1)}, bf16[1,1,256,128]{3,2,1,0:T(8,128)(2,1)S(1)}, u32[]{:S(2)}, u32[]{:S(2)}) collective-permute-start(bf16[1,1,256,128]{3,2,1,0:T(8,128)(2,1)S(1)} %collective-permute-done.9), channel_id=1, source_target_pairs={{2,0},{4,2},{6,4},{8,6},{10,8},{12,10},{14,12},{16,14},{18,16},{20... | collective-permute-start | bytes 196616 | tf_op jit(solution)/shard_map/ppermute | solution.py:22
  37.2 6.4 %collective-permute-start.4 = (bf16[1,1,256,128]{3,2,1,0:T(8,128)(2,1)S(1)}, bf16[1,1,256,128]{3,2,1,0:T(8,128)(2,1)S(1)}, u32[]{:S(2)}, u32[]{:S(2)}) collective-permute-start(bf16[1,1,256,128]{3,2,1,0:T(8,128)(2,1)S(1)} %collective-permute-done.3), channel_id=1, source_target_pairs={{0,2},{2,4},{4,6},{6,8},{8,10},{10,12},{12,14},{14,16},{16,18},{18... | collective-permute-start | bytes 196616 | tf_op jit(solution)/shard_map/ppermute | solution.py:20
  39.1 6.4 %collective-permute-start.11 = (bf16[1,1,256,128]{3,2,1,0:T(8,128)(2,1)S(1)}, bf16[1,1,256,128]{3,2,1,0:T(8,128)(2,1)S(1)}, u32[]{:S(2)}, u32[]{:S(2)}) collective-permute-start(bf16[1,1,256,128]{3,2,1,0:T(8,128)(2,1)S(1)} %collective-permute-done.10), channel_id=1, source_target_pairs={{2,0},{4,2},{6,4},{8,6},{10,8},{12,10},{14,12},{16,14},{18,16},{20... | collective-permute-start | bytes 196616 | tf_op jit(solution)/shard_map/ppermute | solution.py:22
  43.6 6.4 %collective-permute-start.5 = (bf16[1,1,256,128]{3,2,1,0:T(8,128)(2,1)S(1)}, bf16[1,1,256,128]{3,2,1,0:T(8,128)(2,1)S(1)}, u32[]{:S(2)}, u32[]{:S(2)}) collective-permute-start(bf16[1,1,256,128]{3,2,1,0:T(8,128)(2,1)S(1)} %collective-permute-done.4), channel_id=1, source_target_pairs={{0,2},{2,4},{4,6},{6,8},{8,10},{10,12},{12,14},{14,16},{16,18},{18... | collective-permute-start | bytes 196616 | tf_op jit(solution)/shard_map/ppermute | solution.py:20
  45.5 6.4 %collective-permute-start.12 = (bf16[1,1,256,128]{3,2,1,0:T(8,128)(2,1)S(1)}, bf16[1,1,256,128]{3,2,1,0:T(8,128)(2,1)S(1)}, u32[]{:S(2)}, u32[]{:S(2)}) collective-permute-start(bf16[1,1,256,128]{3,2,1,0:T(8,128)(2,1)S(1)} %collective-permute-done.11), channel_id=1, source_target_pairs={{2,0},{4,2},{6,4},{8,6},{10,8},{12,10},{14,12},{16,14},{18,16},{20... | collective-permute-start | bytes 196616 | tf_op jit(solution)/shard_map/ppermute | solution.py:22
  50.0 6.4 %collective-permute-start.6 = (bf16[1,1,256,128]{3,2,1,0:T(8,128)(2,1)S(1)}, bf16[1,1,256,128]{3,2,1,0:T(8,128)(2,1)S(1)}, u32[]{:S(2)}, u32[]{:S(2)}) collective-permute-start(bf16[1,1,256,128]{3,2,1,0:T(8,128)(2,1)S(1)} %collective-permute-done.5), channel_id=1, source_target_pairs={{0,2},{2,4},{4,6},{6,8},{8,10},{10,12},{12,14},{14,16},{16,18},{18... | collective-permute-start | bytes 196616 | tf_op jit(solution)/shard_map/ppermute | solution.py:20
  51.9 6.4 %collective-permute-start.13 = (bf16[1,1,256,128]{3,2,1,0:T(8,128)(2,1)S(1)}, bf16[1,1,256,128]{3,2,1,0:T(8,128)(2,1)S(1)}, u32[]{:S(2)}, u32[]{:S(2)}) collective-permute-start(bf16[1,1,256,128]{3,2,1,0:T(8,128)(2,1)S(1)} %collective-permute-done.12), channel_id=1, source_target_pairs={{2,0},{4,2},{6,4},{8,6},{10,8},{12,10},{14,12},{16,14},{18,16},{20... | collective-permute-start | bytes 196616 | tf_op jit(solution)/shard_map/ppermute | solution.py:22
  56.4 6.4 %collective-permute-start.7 = (bf16[1,1,256,128]{3,2,1,0:T(8,128)(2,1)S(1)}, bf16[1,1,256,128]{3,2,1,0:T(8,128)(2,1)S(1)}, u32[]{:S(2)}, u32[]{:S(2)}) collective-permute-start(bf16[1,1,256,128]{3,2,1,0:T(8,128)(2,1)S(1)} %collective-permute-done.6), channel_id=1, source_target_pairs={{0,2},{2,4},{4,6},{6,8},{8,10},{10,12},{12,14},{14,16},{16,18},{18... | collective-permute-start | bytes 196616 | tf_op jit(solution)/shard_map/ppermute | solution.py:20
  58.3 6.4 %collective-permute-start.14 = (bf16[1,1,256,128]{3,2,1,0:T(8,128)(2,1)S(1)}, bf16[1,1,256,128]{3,2,1,0:T(8,128)(2,1)S(1)}, u32[]{:S(2)}, u32[]{:S(2)}) collective-permute-start(bf16[1,1,256,128]{3,2,1,0:T(8,128)(2,1)S(1)} %collective-permute-done.13), channel_id=1, source_target_pairs={{2,0},{4,2},{6,4},{8,6},{10,8},{12,10},{14,12},{16,14},{18,16},{20... | collective-permute-start | bytes 196616 | tf_op jit(solution)/shard_map/ppermute | solution.py:22
  67.4 68.6 %reduce-scatter.2.cloned.1.call-start = ((), (), s32[]{:S(2)}) async-start(), calls=%async_computation.1 | async-start | bytes 2228224 | tf_op jit(solution)/shard_map/reduce_scatter | solution.py:55
  73.4 35.4 %slice-start = ((s8[4718592]{0:T(1024)(128)(4,1)}), s8[524288]{0:T(1024)(128)(4,1)S(1)}, s32[]{:S(2)}) async-start(s8[4718592]{0:T(1024)(128)(4,1)} %bitcast.193), calls=%async_computation.3 | async-start | bytes 1048576
  102.2 1.9 %copy-start = (bf16[1,2,256,2048]{3,2,0,1:T(8,128)(2,1)S(1)}, bf16[1,2,256,2048]{3,2,0,1:T(8,128)(2,1)}, u32[]{:S(2)}) copy-start(bf16[1,2,256,2048]{3,2,0,1:T(8,128)(2,1)} %all-gather.2.cloned.1.call-done) | copy-start | bytes 6291460
  104.1 4.7 %slice-start.1 = ((s8[4718592]{0:T(1024)(128)(4,1)}), s8[4194304]{0:T(1024)(128)(4,1)S(1)}, s32[]{:S(2)}) async-start(s8[4718592]{0:T(1024)(128)(4,1)} %bitcast.193), calls=%async_computation.4 | async-start | bytes 8388608
Sparse Core Ops, SparseCore 0:
  67.6 34.5 all-gather.1
Sparse Core Ops, SparseCore 1:
  73.1 62.9 reduce-scatter.1
